TPU v7x, 32 devices: a whole 2x2x4 slice. The times are simulated.
32 devices in a mesh: seq: 8 (over z, y), head: 4 (over x, core).
Axes of the slice: x: 2, y: 2, z: 4, core: 2. Of those that a mesh axis runs over, the one named last changes fastest.
Arguments:
- queries: bfloat16 [4096, 6144], P('seq', 'head'), may hold values from -6 to 6
- keys: bfloat16 [4096, 6144], P('seq', 'head'), may hold values from -6 to 6
- values: bfloat16 [4096, 6144], P('seq', 'head'), may hold values from -6 to 6
- attn_out: bfloat16 [4096, 6144], P('seq', 'head'), may hold values from -120 to 120
- out_grad: bfloat16 [4096, 6144], P('seq', 'head'), may hold values from -6 to 6
- norm_gain: float32 [6144], P('head'), may hold values from 0.5 to 2
Outputs:
- query_grad: bfloat16 [4096, 6144], P('seq', 'head')
- key_grad: bfloat16 [4096, 6144], P('seq', 'head')
- value_grad: bfloat16 [4096, 6144], P('seq', 'head')
All inputs are finite; a program needn't handle non-finite values.
Results may differ from a plain program's by a relative error of at most 0.0057.
Values sent between devices are 32-bit elements; how exact they have to be, the bound alone decides.
A program may use at most 128 MiB of HBM per device.

v0:
```python
import math

import jax
import jax.numpy as jnp
from jax import lax
from jax.sharding import PartitionSpec as P

DH = 128
GROUP = 256


EPS = 1e-06


def prefix(part, axis, combine, identity, reverse):
    count = lax.axis_size(axis)
    place = lax.axis_index(axis)
    ahead = count - 1 - place if reverse else place
    gathered = lax.all_gather(part, axis)
    state = jnp.zeros_like(part) + jnp.asarray(identity, part.dtype)

    def one(hop, state):
        source = count - 1 - hop if reverse else hop
        return combine(state, lax.dynamic_index_in_dim(gathered, source, 0, False))

    return lax.fori_loop(0, ahead, one, state)


def add_arrays(earlier, later):
    return earlier + later


def shards(queries, keys, values, attn_out, out_grad, norm_gain):
    tokens_here, width = queries.shape
    heads_here = width // DH
    full_width = width * lax.axis_size("head")
    tokens_all = tokens_here * lax.axis_size("seq")
    factor = 1.0 / math.sqrt(DH * tokens_all)
    outf = attn_out.astype(jnp.float32)
    scaled = norm_gain[None, :] * out_grad.astype(jnp.float32)
    square_part = jnp.sum(outf * outf, axis=-1)
    cross_part = jnp.sum(scaled * outf, axis=-1)
    square_sum, cross_sum = lax.psum((square_part, cross_part), "head")
    rms = jnp.sqrt(square_sum / full_width + EPS)
    grad_out = (
        scaled / rms[:, None] - outf * (cross_sum / (full_width * rms**3))[:, None]
    ).astype(jnp.bfloat16)
    blocks = tokens_here // GROUP
    shape = (blocks, GROUP, heads_here, DH)
    qb = queries.reshape(shape)
    kb = keys.reshape(shape)
    vb = values.reshape(shape)
    gb = grad_out.reshape(shape)
    f32 = jnp.float32
    kv_terms = jnp.einsum("ctni,ctnj->cnij", kb, vb, preferred_element_type=f32)
    qg_terms = jnp.einsum("ctni,ctnj->cnij", qb, gb, preferred_element_type=f32)
    kv_sum = jnp.sum(kv_terms, axis=0)
    qg_sum = jnp.sum(qg_terms, axis=0)
    zeros = jnp.zeros_like(kv_sum)
    before = prefix(kv_sum, "seq", add_arrays, zeros, False)
    after = prefix(qg_sum, "seq", add_arrays, zeros, True)
    fwd_state = (before[None] + jnp.cumsum(kv_terms, axis=0) - kv_terms).astype(jnp.bfloat16)
    bwd_state = (after[None] + qg_sum[None] - jnp.cumsum(qg_terms, axis=0)).astype(jnp.bfloat16)
    causal = (jnp.arange(GROUP)[:, None] >= jnp.arange(GROUP)[None, :])[None, None]
    scores = jnp.einsum("ctni,csni->cnts", qb, kb, preferred_element_type=f32)
    scores = jnp.where(causal, scores, 0.0).astype(jnp.bfloat16)
    prods = jnp.einsum("ctnj,csnj->cnts", gb, vb, preferred_element_type=f32)
    prods = jnp.where(causal, prods, 0.0).astype(jnp.bfloat16)
    qgrad = jnp.einsum("cnts,csni->ctni", prods, kb, preferred_element_type=f32)
    qgrad = qgrad + jnp.einsum("ctnj,cnij->ctni", gb, fwd_state, preferred_element_type=f32)
    kgrad = jnp.einsum("cnts,ctni->csni", prods, qb, preferred_element_type=f32)
    kgrad = kgrad + jnp.einsum("csnj,cnij->csni", vb, bwd_state, preferred_element_type=f32)
    vgrad = jnp.einsum("cnts,ctnj->csnj", scores, gb, preferred_element_type=f32)
    vgrad = vgrad + jnp.einsum("csni,cnij->csnj", kb, bwd_state, preferred_element_type=f32)
    query_grad = (qgrad * factor).astype(jnp.bfloat16).reshape(tokens_here, width)
    key_grad = (kgrad * factor).astype(jnp.bfloat16).reshape(tokens_here, width)
    value_grad = (vgrad * factor).astype(jnp.bfloat16).reshape(tokens_here, width)
    return (query_grad, key_grad, value_grad)


def solution(mesh):
    in_specs = (
        P("seq", "head"),
        P("seq", "head"),
        P("seq", "head"),
        P("seq", "head"),
        P("seq", "head"),
        P("head"),
    )
    out_specs = (P("seq", "head"), P("seq", "head"), P("seq", "head"))
    return jax.shard_map(shards, mesh=mesh, in_specs=in_specs, out_specs=out_specs, check_vma=False)
```

profile of v0, /device:TPU:0, one launch (start us, length us, event | category | flops | bytes accessed | tf_op | source)
XLA Modules:
  0.0 249.8 jit_solution(8065300581111332722)
XLA Ops:
  7.2 2.8 %fusion = (f32[512]{0:T(512)S(1)}, f32[512]{0:T(512)S(1)}) fusion(bf16[512,1536]{1,0:T(8,128)(2,1)} %param.13, bf16[512,1536]{1,0:T(8,128)(2,1)} %param.14, f32[1536]{0:T(1024)} %param.15), kind=kLoop, calls=%fused_computation.7 | loop fusion | flops 5504000 | bytes 3155968 | tf_op jit(solution)/shard_map/reduce_sum | solution.py:41
  10.0 8.3 %all-reduce = (f32[512]{0:T(512)S(1)}, f32[512]{0:T(512)S(1)}) all-reduce(f32[512]{0:T(512)S(1)} %get-tuple-element.91, f32[512]{0:T(512)S(1)} %get-tuple-element.90), channel_id=1, replica_groups=mesh['seq'=8,'head'=4] {'head'}, use_global_device_ids=true, to_apply=%region_3.0 | all-reduce | flops 1024 | bytes 8192 | tf_op jit(solution)/shard_map/psum | solution.py:43
  18.4 2.1 fusion.3
  20.5 2.1 reshape.59
  22.7 3.4 %copy.67 = bf16[2,256,12,128]{1,3,2,0:T(8,128)(2,1)S(1)} copy(bf16[2,256,12,128]{3,2,1,0:T(8,128)(2,1)} %reshape.59) | data formatting | bytes 3145728 | tf_op jit(solution)/shard_map/reshape | solution.py:53
  26.1 2.2 reshape.58
  28.3 3.4 %bitcast_reduce_fusion = (f32[12,128,128]{1,2,0:T(8,128)S(1)}, f32[2,12,128,128]{3,2,1,0:T(8,128)}) fusion(bf16[2,256,12,128]{1,3,2,0:T(8,128)(2,1)S(1)} %copy.67, bf16[2,256,12,128]{3,2,1,0:T(8,128)(2,1)} %reshape.58), kind=kOutput, calls=%fused_computation.30 | convolution fusion | flops 201523200 | bytes 5505024 | tf_op jit(solution)/shard_map/ctni,ctnj->cnij/dot_general | solution.py:56
  32.9 4.0 %reshape.57 = bf16[2,256,12,128]{3,2,1,0:T(8,128)(2,1)} reshape(bf16[512,1536]{1,0:T(8,128)(2,1)} %param.12) | data formatting | bytes 3145728 | tf_op jit(solution)/shard_map/reshape | solution.py:52
  36.9 4.0 %reshape.60 = bf16[2,256,12,128]{3,2,1,0:T(8,128)(2,1)} reshape(bf16[512,1536]{1,0:T(8,128)(2,1)} %param.11) | data formatting | bytes 3145728 | tf_op jit(solution)/shard_map/reshape | solution.py:51
  40.9 3.4 %copy.59 = bf16[2,256,12,128]{1,3,2,0:T(8,128)(2,1)S(1)} copy(bf16[2,256,12,128]{3,2,1,0:T(8,128)(2,1)} %reshape.60) | data formatting | bytes 3145728 | tf_op jit(solution)/shard_map/reshape | solution.py:51
  44.3 4.3 %fusion.33 = (f32[12,128,128]{2,1,0:T(8,128)}, f32[2,12,128,128]{3,2,1,0:T(8,128)}) fusion(bf16[2,256,12,128]{1,3,2,0:T(8,128)(2,1)S(1)} %copy.59, bf16[2,256,12,128]{3,2,1,0:T(8,128)(2,1)} %reshape.57), kind=kOutput, calls=%fused_computation.49 | convolution fusion | flops 201523200 | bytes 5505024 | tf_op jit(solution)/shard_map/ctni,ctnj->cnij/dot_general | solution.py:55
  48.7 2.9 %select_convert_fusion.1 = bf16[2,12,256,256]{3,2,1,0:T(8,128)(2,1)S(1)} fusion(pred[256,256]{1,0:T(8,128)(4,1)S(1)} %iota_compare_fusion, bf16[2,256,12,128]{1,3,2,0:T(8,128)(2,1)S(1)} %copy.67, bf16[2,256,12,128]{3,2,1,0:T(8,128)(2,1)} %reshape.57), kind=kOutput, calls=%fused_computation.3 | convolution fusion | flops 405798912 | bytes 6356992 | tf_op jit(solution)/shard_map/ctnj,csnj->cnts/dot_general | solution.py:67
  51.6 2.8 %fusion.24 = f32[2,12,256,128]{3,2,1,0:T(8,128)} fusion(bf16[2,12,256,256]{3,2,1,0:T(8,128)(2,1)S(1)} %select_convert_fusion.1, bf16[2,256,12,128]{3,2,1,0:T(8,128)(2,1)S(1)} %copy-done.4), kind=kOutput, calls=%fused_computation.37 | convolution fusion | flops 402653184 | bytes 7864320 | tf_op jit(solution)/shard_map/cnts,ctni->csni/dot_general | solution.py:71
  54.4 2.6 %fusion.34 = f32[2,12,256,128]{3,2,1,0:T(8,128)} fusion(bf16[2,12,256,256]{3,2,1,0:T(8,128)(2,1)S(1)} %select_convert_fusion.1, bf16[2,256,12,128]{1,3,2,0:T(8,128)(2,1)S(1)} %copy.59), kind=kOutput, calls=%fused_computation.50 | convolution fusion | flops 402653184 | bytes 7864320 | tf_op jit(solution)/shard_map/cnts,csni->ctni/dot_general | solution.py:69
  57.0 4.7 %fusion.4 = f32[2,12,128,256]{3,2,1,0:T(8,128)} fusion(bf16[2,256,12,128]{1,3,2,0:T(8,128)(2,1)S(1)} %copy.67, pred[256,256]{1,0:T(8,128)(4,1)S(1)} %iota_compare_fusion, bf16[2,256,12,128]{1,3,2,0:T(8,128)(2,1)S(1)} %copy.59, bf16[2,256,12,128]{3,2,1,0:T(8,128)(2,1)} %reshape.58), kind=kOutput, calls=%fused_computation.11 | convolution fusion | flops 808452096 | bytes 7929856 | tf_op jit(solution)/shard_map/cnts,ctnj->csnj/dot_general | solution.py:73
  61.7 70.7 %all-gather.7.cloned.1.call-done = f32[96,128,128]{2,1,0:T(8,128)} async-done(((f32[12,128,128]{2,1,0:T(8,128)}), f32[96,128,128]{2,1,0:T(8,128)}) %all-gather.7.cloned.1.call-update) | async-done | bytes 6291472 | tf_op jit(solution)/shard_map/all_gather | solution.py:19
  132.4 9.8 %while.23 = (s32[]{:T(128)}, f32[12,128,128]{2,1,0:T(8,128)S(1)}, s32[]{:T(128)}, f32[8,12,128,128]{3,2,1,0:T(8,128)}, s32[]{:T(128)}, /*index=5*/s32[]{:T(128)}, s32[]{:T(128)}, s32[]{:T(128)}) while((s32[]{:T(128)}, f32[12,128,128]{2,1,0:T(8,128)S(1)}, s32[]{:T(128)}, f32[8,12,128,128]{3,2,1,0:T(8,128)}, s32[]{:T(128)}, ...), condition=%wide.region_10.11_spmd, body=%wide.region_9.10_spmd.sunk | while | flops 196614 | bytes 2359431 | solution.py:26
  132.5 1.3 bitcast_add_fusion.7
  133.8 1.3 bitcast_add_fusion.7
  135.2 1.3 bitcast_add_fusion.7
  136.5 1.3 bitcast_add_fusion.7
  137.9 1.3 bitcast_add_fusion.7
  139.3 1.4 bitcast_add_fusion.7
  140.7 1.4 bitcast_add_fusion.7
  143.4 1.4 add.66
  144.8 1.8 fusion.17
  147.8 2.4 copy.88
  150.8 3.0 %copy.89 = bf16[2,256,12,128]{3,2,1,0:T(8,128)(2,1)} copy(bf16[2,256,12,128]{1,3,2,0:T(8,128)(2,1)S(1)} %fusion.15) | data formatting | bytes 3145728
  153.9 77.9 %all-gather.5.cloned.1.call-done = f32[96,128,128]{2,1,0:T(8,128)} async-done(((f32[12,128,128]{2,1,0:T(8,128)}), f32[96,128,128]{2,1,0:T(8,128)}) %all-gather.5.cloned.1.call-update) | async-done | bytes 6291472 | tf_op jit(solution)/shard_map/all_gather | solution.py:19
  231.9 1.4 copy-done.2
  237.6 1.6 copy.124
  239.7 3.2 %copy_bitcast_fusion = (bf16[512,1536]{1,0:T(8,128)(2,1)}, bf16[512,1536]{1,0:T(8,128)(2,1)}) fusion(bf16[64,8,12,128]{3,2,1,0:T(8,128)(2,1)S(1)} %bitcast.62, bf16[64,8,12,128]{3,2,1,0:T(8,128)(2,1)S(1)} %bitcast.61), kind=kLoop, calls=%fused_computation.26 | loop fusion | bytes 6291456
  (45 shorter events, 9.3 us)
Async XLA Ops:
  7.2 11.2 %copy-start.11 = (bf16[512,1536]{1,0:T(8,128)(2,1)S(1)}, bf16[512,1536]{1,0:T(8,128)(2,1)}, u32[]{:S(2)}) copy-start(bf16[512,1536]{1,0:T(8,128)(2,1)} %param.13) | copy-start | bytes 4718596
  7.2 11.2 %copy-start.14 = (f32[1536]{0:T(1024)S(1)}, f32[1536]{0:T(1024)}, u32[]{:S(2)}) copy-start(f32[1536]{0:T(1024)} %param.15) | copy-start | bytes 18436
  7.2 125.2 %all-gather.7.cloned.1.call-start = ((), (), s32[]{:S(2)}) async-start(), calls=%async_computation.1 | async-start | bytes 7077888 | tf_op jit(solution)/shard_map/all_gather | solution.py:19
  22.7 3.4 %copy-start.13 = (bf16[512,1536]{1,0:T(8,128)(2,1)S(1)}, bf16[512,1536]{1,0:T(8,128)(2,1)}, u32[]{:S(2)}) copy-start(bf16[512,1536]{1,0:T(8,128)(2,1)} %param.10) | copy-start | bytes 4718596
  26.1 30.9 %copy-start = (bf16[2,256,12,128]{1,3,2,0:T(8,128)(2,1)}, bf16[2,256,12,128]{1,3,2,0:T(8,128)(2,1)S(1)}, u32[]{:S(2)}) copy-start(bf16[2,256,12,128]{1,3,2,0:T(8,128)(2,1)S(1)} %copy.67) | copy-start | bytes 4718596
  31.7 5.3 %copy-start.9 = (f32[12,128,128]{1,2,0:T(8,128)}, f32[12,128,128]{1,2,0:T(8,128)S(1)}, u32[]{:S(2)}) copy-start(f32[12,128,128]{1,2,0:T(8,128)S(1)} %get-tuple-element.114) | copy-start | bytes 2359300
  32.9 198.9 %all-gather.5.cloned.1.call-start = ((), (), s32[]{:S(2)}) async-start(), calls=%async_computation | async-start | bytes 7077888 | tf_op jit(solution)/shard_map/all_gather | solution.py:19
  48.7 2.9 %copy-start.4 = (bf16[2,256,12,128]{3,2,1,0:T(8,128)(2,1)S(1)}, bf16[2,256,12,128]{3,2,1,0:T(8,128)(2,1)}, u32[]{:S(2)}) copy-start(bf16[2,256,12,128]{3,2,1,0:T(8,128)(2,1)} %reshape.58) | copy-start | bytes 4718596
  142.3 1.2 copy-start.10
  143.4 3.2 %copy-start.6 = (f32[2,12,256,128]{3,2,1,0:T(8,128)S(1)}, f32[2,12,256,128]{3,2,1,0:T(8,128)}, u32[]{:S(2)}) copy-start(f32[2,12,256,128]{3,2,1,0:T(8,128)} %fusion.24) | copy-start | bytes 9437188
  144.8 2.3 copy-start.3
  147.8 2.4 copy-start.12
  231.9 1.4 copy-start.2
  233.3 1.4 copy-start.1
  233.3 2.4 copy-start.5
  236.4 2.7 %copy-start.8 = (bf16[2,256,12,128]{3,2,1,0:T(8,128)(2,1)S(1)}, bf16[2,256,12,128]{3,2,1,0:T(8,128)(2,1)}, u32[]{:S(2)}) copy-start(bf16[2,256,12,128]{3,2,1,0:T(8,128)(2,1)} %copy.89) | copy-start | bytes 4718596
  237.5 2.2 copy-start.7
Sparse Core Ops, SparseCore 0:
  33.0 99.3 all-gather.6
  134.6 97.1 all-gather.4
where the time goes:
time: 255 us; the launch traced here: 250 us
  waiting for transfers between devices  149 us (58%)
  local copies, waits for them, and re-layouts  37.5 us (15%)
  matrix products  22.9 us (9%)
  other arithmetic  17.8 us (7%)
  between operations  14.3 us (6%)
  blocking collectives  8.34 us (3%)
    all_gather x2, waiting for transfers between devices, prefix(): gathered = lax.all_gather(part, axis)  149 us
    unnamed x35, local copies, waits for them, and re-layouts  16 us
    add x7, other arithmetic, add_arrays(): return earlier + later  9.45 us
    psum x1, blocking collectives, shards(): square_sum, cross_sum = lax.psum((square_part, cross_part), 'head')  8.34 us
    reshape x2, local copies, waits for them, and re-layouts, shards(): kb = keys.reshape(shape)  7.36 us
    reshape x2, local copies, waits for them, and re-layouts, shards(): gb = grad_out.reshape(shape)  5.54 us
  transfers between devices with their start and end apart: 2, of which 2 were waited for; matrix products, arithmetic and copies ran while one was open for 20% of the time, Pallas kernels for 0%

commit v1 on v0

v1 whole, which is shorter than its diff:
```python
import functools
import math

import jax
import jax.numpy as jnp
from jax import lax
from jax.experimental import pallas as pl
from jax.experimental.pallas import tpu as pltpu
from jax.sharding import PartitionSpec as P

DH = 128
GROUP = 256
EPS = 1e-06
MESH = pl.DeviceIdType.MESH
F32 = jnp.float32
BF16 = jnp.bfloat16
LAG = 2


def dot(a, b, ca, cb):
    return lax.dot_general(a, b, (((ca,), (cb,)), ((), ())), preferred_element_type=F32)


def split_seq(count):
    inner = 1
    while inner * inner * 4 <= count:
        inner *= 2
    while count % inner:
        inner //= 2
    return count // inner, inner


def kernel(
    cfg,
    q_hbm, k_hbm, v_hbm, o_hbm, d_hbm, gain_ref,
    qg_out, kg_out, vg_out,
    q_ref, k_ref, v_ref, o_ref, d_ref,
    acc_q, acc_k, acc_v, terms, slots, zin, inc, sums,
    load_sem, sum_send, sum_recv, y_send, y_recv, z_send, z_recv,
):
    zs, ys, hs, heads, ch, raw, rows, full_width, factor = cfg
    n = heads // ch
    blocks = rows // GROUP
    seq = lax.axis_index("seq")
    mine = lax.axis_index("head")
    z = seq // ys
    y = seq % ys
    hops = (z, zs - 1 - z)

    loads = [
        pltpu.make_async_copy(src, dst, load_sem.at[i])
        for i, (src, dst) in enumerate(
            ((k_hbm, k_ref), (v_hbm, v_ref), (o_hbm, o_ref), (d_hbm, d_ref), (q_hbm, q_ref))
        )
    ]
    for load in loads:
        load.start()

    barrier = pltpu.get_barrier_semaphore()

    def greet(s, h):
        pl.semaphore_signal(barrier, inc=1, device_id=(s, h), device_id_type=MESH)

    for d in range(1, hs):
        greet(seq, lax.rem(mine + d, hs))
    for d in range(1, ys):
        greet(z * ys + lax.rem(y + d, ys), mine)

    @pl.when(z > 0)
    def _():
        greet(seq - ys, mine)

    @pl.when(z < zs - 1)
    def _():
        greet(seq + ys, mine)

    for kind in range(2):

        @pl.when(hops[kind] == 0)
        def _():
            zin[kind] = jnp.zeros_like(zin[kind])

    def chunk(c):
        return pl.ds(c * ch, ch)

    def lanes(h):
        return pl.ds(pl.multiple_of(h * DH, DH), DH)

    def toks(b):
        return slice(b * GROUP, (b + 1) * GROUP)

    def y_copy(kind, src, c, d):
        other = lax.rem(y + d, ys)
        return pltpu.make_async_remote_copy(
            src_ref=src.at[chunk(c)],
            dst_ref=slots.at[kind, y, chunk(c)],
            send_sem=y_send.at[kind, d - 1, c],
            recv_sem=y_recv.at[kind, y, c],
            device_id=(z * ys + other, mine),
            device_id_type=MESH,
        )

    def y_arrive(kind, c, d):
        other = lax.rem(y + d, ys)
        pltpu.make_async_remote_copy(
            src_ref=slots.at[kind, other, chunk(c)],
            dst_ref=slots.at[kind, other, chunk(c)],
            send_sem=y_send.at[kind, d - 1, c],
            recv_sem=y_recv.at[kind, other, c],
            device_id=(z * ys + other, mine),
            device_id_type=MESH,
        ).wait_recv()

    def z_copy(kind, c):
        return pltpu.make_async_remote_copy(
            src_ref=inc.at[kind, chunk(c)],
            dst_ref=zin.at[kind, chunk(c)],
            send_sem=z_send.at[kind, c],
            recv_sem=z_recv.at[kind, c],
            device_id=(seq + (ys if kind == 0 else -ys), mine),
            device_id_type=MESH,
        )

    def later(kind, other):
        return other > y if kind == 0 else other < y

    def own_terms(kind, a_ref, b_ref):
        def one(c, carry):
            for i in range(ch):
                h = c * ch + i
                total = None
                for b in range(blocks):
                    part = dot(a_ref[toks(b), lanes(h)], b_ref[toks(b), lanes(h)], 0, 0)
                    terms[kind, b, h] = part
                    total = part if total is None else total + part
                slots[kind, y, h] = total

            @pl.when(c < raw)
            def _():
                for d in range(1, ys):
                    y_copy(kind, slots.at[kind, y], c, d).start()

            return carry

        lax.fori_loop(0, n, one, 0)

    def step(kind, t):
        place = t - hops[kind]

        @pl.when((place >= 0) & (place < n))
        def _():
            c = lax.rem(place + raw, n)

            @pl.when(hops[kind] > 0)
            def _():
                z_copy(kind, c).wait_recv()

            @pl.when(place >= n - raw)
            def _():
                for d in range(1, ys):
                    y_arrive(kind, c, d)
                total = zin[kind, chunk(c)]
                for s in range(ys):
                    total = total + slots[kind, s, chunk(c)]
                inc[kind, chunk(c)] = total

            @pl.when(place < n - raw)
            def _():
                inc[kind, chunk(c)] = zin[kind, chunk(c)] + slots[kind, y, chunk(c)]
                for d in range(1, ys):
                    other = lax.rem(y + d, ys)

                    @pl.when(later(kind, other))
                    def _():
                        y_copy(kind, inc.at[kind], c, d).start()

                    @pl.when(jnp.logical_not(later(kind, other)))
                    def _():
                        y_copy(kind, zin.at[kind], c, d).start()

            @pl.when(hops[kind] < zs - 1)
            def _():
                z_copy(kind, c).start()

    loads[0].wait()
    loads[1].wait()
    peers = hs - 1 + ys - 1 + jnp.where(z > 0, 1, 0) + jnp.where(z < zs - 1, 1, 0)
    pl.semaphore_wait(barrier, peers)
    own_terms(0, k_ref, v_ref)
    step(0, 0)

    loads[2].wait()
    loads[3].wait()
    tile = 128
    for r in range(rows // tile):
        rs = slice(r * tile, (r + 1) * tile)

        def partial(h, carry):
            sq, cr = carry
            of = o_ref[rs, lanes(h)].astype(F32)
            sc = gain_ref[0:1, lanes(h)] * d_ref[rs, lanes(h)].astype(F32)
            return sq + of * of, cr + sc * of

        zero = jnp.zeros((tile, DH), F32)
        sq, cr = lax.fori_loop(0, heads, partial, (zero, zero))
        sq = jnp.sum(sq.T, axis=0, keepdims=True)
        cr = jnp.sum(cr.T, axis=0, keepdims=True)
        sums[mine, 0:4, rs] = jnp.broadcast_to(sq, (4, tile))
        sums[mine, 4:8, rs] = jnp.broadcast_to(cr, (4, tile))

    def sum_copy(slot, d):
        return pltpu.make_async_remote_copy(
            src_ref=sums.at[slot],
            dst_ref=sums.at[slot],
            send_sem=sum_send.at[d - 1],
            recv_sem=sum_recv.at[slot],
            device_id=(seq, lax.rem(mine + d, hs)),
            device_id_type=MESH,
        )

    for d in range(1, hs):
        sum_copy(mine, d).start()
    for t in range(1, LAG):
        step(0, t)
    for d in range(1, hs):
        sum_copy(lax.rem(mine + d, hs), d).wait_recv()
    total = sums[0]
    for s in range(1, hs):
        total = total + sums[s]
    rms = jnp.sqrt(total[0:1] / full_width + EPS)
    inv_row = 1.0 / rms
    coef_row = total[4:5] / (full_width * (rms * rms * rms))
    for r in range(rows // tile):
        rs = slice(r * tile, (r + 1) * tile)
        inv = jnp.broadcast_to(inv_row[:, rs], (tile, tile)).T
        coef = jnp.broadcast_to(coef_row[:, rs], (tile, tile)).T

        def normed(h, carry):
            of = o_ref[rs, lanes(h)].astype(F32)
            sc = gain_ref[0:1, lanes(h)] * d_ref[rs, lanes(h)].astype(F32)
            d_ref[rs, lanes(h)] = (sc * inv - of * coef).astype(BF16)
            return carry

        lax.fori_loop(0, heads, normed, 0)

    loads[4].wait()
    own_terms(1, q_ref, d_ref)

    def local(c):
        row = lax.broadcasted_iota(jnp.int32, (GROUP, GROUP), 0)
        col = lax.broadcasted_iota(jnp.int32, (GROUP, GROUP), 1)
        for i in range(ch):
            h = c * ch + i
            for b in range(blocks):
                qb = q_ref[toks(b), lanes(h)]
                kb = k_ref[toks(b), lanes(h)]
                vb = v_ref[toks(b), lanes(h)]
                gb = d_ref[toks(b), lanes(h)]
                prods = jnp.where(row >= col, dot(gb, vb, 1, 1), 0.0).astype(BF16)
                acc_q[toks(b), lanes(h)] = dot(prods, kb, 1, 0)
                prods_t = jnp.where(col >= row, dot(vb, gb, 1, 1), 0.0).astype(BF16)
                acc_k[toks(b), lanes(h)] = dot(prods_t, qb, 1, 0)
                scores_t = jnp.where(col >= row, dot(kb, qb, 1, 1), 0.0).astype(BF16)
                acc_v[toks(b), lanes(h)] = dot(scores_t, gb, 1, 0)

    def turn(t, carry):
        step(0, t)
        step(1, t - LAG)

        @pl.when(t - LAG < n)
        def _():
            local(t - LAG)

        return carry

    lax.fori_loop(LAG, n + zs - 1 + LAG, turn, 0)

    def finish(c, carry):
        @pl.when(c >= raw)
        def _():
            for kind in range(2):
                for d in range(1, ys):
                    y_arrive(kind, c, d)

        for i in range(ch):
            h = c * ch + i
            ends = []
            for kind in range(2):
                total = zin[kind, h]
                for d in range(1, ys):
                    other = lax.rem(y + d, ys)
                    used = jnp.logical_or(c >= raw, jnp.logical_not(later(kind, other)))
                    total = total + jnp.where(used, slots[kind, other, h], 0.0)
                ends.append(total)
            fwd, bwd = [ends[0]], [ends[1]]
            for b in range(blocks - 1):
                fwd.append(fwd[-1] + terms[0, b, h])
                bwd.insert(0, bwd[0] + terms[1, blocks - 1 - b, h])
            for b in range(blocks):
                at = (toks(b), lanes(h))
                kb, vb, gb = k_ref[at], v_ref[at], d_ref[at]
                fs, bs = fwd[b].astype(BF16), bwd[b].astype(BF16)
                qg_out[at] = ((acc_q[at] + dot(gb, fs, 1, 1)) * factor).astype(BF16)
                kg_out[at] = ((acc_k[at] + dot(vb, bs, 1, 1)) * factor).astype(BF16)
                vg_out[at] = ((acc_v[at] + dot(kb, bs, 1, 0)) * factor).astype(BF16)
        return carry

    lax.fori_loop(0, n, finish, 0)

    for d in range(1, hs):
        sum_copy(mine, d).wait_send()

    def sent(c, carry):
        for kind in range(2):
            for d in range(1, ys):
                y_copy(kind, inc.at[kind], c, d).wait_send()

            @pl.when(hops[kind] < zs - 1)
            def _():
                z_copy(kind, c).wait_send()

        return carry

    lax.fori_loop(0, n, sent, 0)


def shards(sizes, queries, keys, values, attn_out, out_grad, norm_gain):
    seqs, hs = sizes
    zs, ys = split_seq(seqs)
    rows, width = queries.shape
    heads = width // DH
    blocks = rows // GROUP
    ch = 2 if heads % 2 == 0 else 1
    n = heads // ch
    raw = n // 3
    factor = 1.0 / math.sqrt(DH * rows * seqs)
    cfg = (zs, ys, hs, heads, ch, raw, rows, width * hs, factor)
    big = pltpu.VMEM((rows, width), BF16)
    acc = pltpu.VMEM((rows, width), F32)
    state = (heads, DH, DH)
    out = jax.ShapeDtypeStruct((rows, width), BF16)
    dma = pltpu.SemaphoreType.DMA
    flops = 2 * heads * blocks * (6 * GROUP * GROUP * DH + 5 * GROUP * DH * DH)
    return pl.pallas_call(
        functools.partial(kernel, cfg),
        out_shape=(out, out, out),
        in_specs=[pl.BlockSpec(memory_space=pl.ANY)] * 5 + [pl.BlockSpec(memory_space=pltpu.VMEM)],
        out_specs=[pl.BlockSpec(memory_space=pltpu.VMEM)] * 3,
        scratch_shapes=[
            big, big, big, big, big,
            acc, acc, acc,
            pltpu.VMEM((2, blocks) + state, F32),
            pltpu.VMEM((2, ys) + state, F32),
            pltpu.VMEM((2,) + state, F32),
            pltpu.VMEM((2,) + state, F32),
            pltpu.VMEM((hs, 8, rows), F32),
            dma((5,)),
            dma((hs - 1,)),
            dma((hs,)),
            dma((2, ys - 1, n)),
            dma((2, ys, n)),
            dma((2, n)),
            dma((2, n)),
        ],
        cost_estimate=pl.CostEstimate(
            flops=flops, bytes_accessed=8 * rows * width * 2, transcendentals=0
        ),
        compiler_params=pltpu.CompilerParams(
            collective_id=0, has_side_effects=True, vmem_limit_bytes=42 * 1024 * 1024
        ),
    )(queries, keys, values, attn_out, out_grad, norm_gain[None, :])


def solution(mesh):
    sizes = (mesh.shape["seq"], mesh.shape["head"])
    spec = P("seq", "head")
    return jax.shard_map(
        functools.partial(shards, sizes),
        mesh=mesh,
        in_specs=(spec,) * 5 + (P("head"),),
        out_specs=(spec,) * 3,
        check_vma=False,
    )
```

time: 255 us -> 60.6 us (0.24); the launches traced: 250 us -> 60.3 us
  waiting for transfers between devices: 149 us -> 0 us
  Pallas kernels: 0 us -> 49.9 us
  local copies, waits for them, and re-layouts: 37.5 us -> 9.76 us
  matrix products: 22.9 us -> 0 us
  other arithmetic: 17.8 us -> 0 us
  between operations: 14.3 us -> 0.64 us
  blocking collectives: 8.34 us -> 0 us
    all_gather x2 -> x0, waiting for transfers between devices: 149 us -> none  [prefix(): gathered = lax.all_gather(part, axis)]
    pallas_call x0 -> x1, Pallas kernels: none -> 49.9 us  [shards(): pl.pallas_call(functools.partial(kernel, cfg), out_shape=(out, out, out),...]
    dot_general x9 -> x0, matrix products: 22.9 us -> none  [the longest x1 4.69 us: shards(): jnp.einsum('cnts,ctnj->csnj', scores, gb, preferred_element_type=f32)]
    reshape x6 -> x0, local copies, waits for them, and re-layouts: 19.1 us -> none  [the longest x2 7.36 us: shards(): kb = keys.reshape(shape)]
    add x8 -> x0, other arithmetic: 10.8 us -> none  [the longest x7 9.45 us: add_arrays(): return earlier + later]
    psum x1 -> x0, blocking collectives: 8.34 us -> none  [shards(): square_sum, cross_sum = lax.psum((square_part, cross_part), 'head')]
    unnamed x35 -> x11, local copies, waits for them, and re-layouts: 16 us -> 9.06 us
    reduce_sum x1 -> x0, other arithmetic: 2.79 us -> none  [shards(): square_part = jnp.sum(outf * outf, axis=-1)]
  transfers between devices with their start and end apart: 2 -> 0, of which waited for: 2 -> 0; matrix products, arithmetic and copies ran while one was open for 20% -> 0% of each run, Pallas kernels for 0% -> 0%
where the time goes in v1:
time: 60.6 us; the launch traced here: 60.3 us
  Pallas kernels  49.9 us (82%)
  local copies, waits for them, and re-layouts  9.76 us (16%)
  between operations  0.64 us (1%)
    pallas_call x1, Pallas kernels, shards(): pl.pallas_call(functools.partial(kernel, cfg), out_shape=(out, out, out),...  49.9 us
    unnamed x11, local copies, waits for them, and re-layouts  9.06 us

profile of v1, /device:TPU:0, one launch (start us, length us, event | category | flops | bytes accessed | tf_op | source)
XLA Modules:
  0.0 60.3 jit_solution(11038956438728641107)
XLA Ops:
  0.6 0.7 %broadcast_in_dim.3.gain_ref = f32[1,1536]{1,0:T(1,128)S(1)} reshape(f32[1536]{0:T(1024)} %param.11) | data formatting | bytes 12288 | tf_op jit(solution)/shard_map/broadcast_in_dim | solution.py:371
  1.3 0.0 copy-start
  1.3 1.4 %copy-done = bf16[512,1536]{1,0:T(8,128)(2,1)S(1)} copy-done((bf16[512,1536]{1,0:T(8,128)(2,1)S(1)}, bf16[512,1536]{1,0:T(8,128)(2,1)}, u32[]{:S(2)}) %copy-start) | copy-done | bytes 1572888
  2.7 0.0 copy-start.1
  2.7 1.4 %copy-done.1 = bf16[512,1536]{1,0:T(8,128)(2,1)S(1)} copy-done((bf16[512,1536]{1,0:T(8,128)(2,1)S(1)}, bf16[512,1536]{1,0:T(8,128)(2,1)}, u32[]{:S(2)}) %copy-start.1) | copy-done | bytes 1572888
  4.1 0.0 copy-start.2
  4.2 1.4 %copy-done.2 = bf16[512,1536]{1,0:T(8,128)(2,1)S(1)} copy-done((bf16[512,1536]{1,0:T(8,128)(2,1)S(1)}, bf16[512,1536]{1,0:T(8,128)(2,1)}, u32[]{:S(2)}) %copy-start.2) | copy-done | bytes 1572888
  5.6 0.0 copy-start.3
  5.6 1.4 %copy-done.3 = bf16[512,1536]{1,0:T(8,128)(2,1)S(1)} copy-done((bf16[512,1536]{1,0:T(8,128)(2,1)S(1)}, bf16[512,1536]{1,0:T(8,128)(2,1)}, u32[]{:S(2)}) %copy-start.3) | copy-done | bytes 1572888
  7.0 49.9 %shard_map.85 = (bf16[512,1536]{1,0:T(8,128)(2,1)S(1)}, bf16[512,1536]{1,0:T(8,128)(2,1)S(1)}, bf16[512,1536]{1,0:T(8,128)(2,1)S(1)}) custom-call(bf16[512,1536]{1,0:T(8,128)(2,1)S(1)} %copy-done, bf16[512,1536]{1,0:T(8,128)(2,1)S(1)} %copy-done.1, bf16[512,1536]{1,0:T(8,128)(2,1)S(1)} %copy-done.2, bf16[512,1536]{1,0:T(8,128)(2,1)S(1)} %copy-done.3, ...), custom_call_target="tpu_custom_call" | custom-call | flops 3422552064 | bytes 12582912 | tf_op jit(solution)/shard_map/pallas_call | solution.py:344
  56.9 1.1 %copy.12 = bf16[512,1536]{1,0:T(8,128)(2,1)} copy(bf16[512,1536]{1,0:T(8,128)(2,1)S(1)} %get-tuple-element.6) | data formatting | bytes 3145728
  58.0 1.1 %copy.13 = bf16[512,1536]{1,0:T(8,128)(2,1)} copy(bf16[512,1536]{1,0:T(8,128)(2,1)S(1)} %get-tuple-element.7) | data formatting | bytes 3145728
  59.2 1.1 %copy.14 = bf16[512,1536]{1,0:T(8,128)(2,1)} copy(bf16[512,1536]{1,0:T(8,128)(2,1)S(1)} %get-tuple-element.8) | data formatting | bytes 3145728
Async XLA Ops:
  1.3 1.4 %copy-start = (bf16[512,1536]{1,0:T(8,128)(2,1)S(1)}, bf16[512,1536]{1,0:T(8,128)(2,1)}, u32[]{:S(2)}) copy-start(bf16[512,1536]{1,0:T(8,128)(2,1)} %q_hbm.1) | copy-start | bytes 4718596
  2.7 1.4 %copy-start.1 = (bf16[512,1536]{1,0:T(8,128)(2,1)S(1)}, bf16[512,1536]{1,0:T(8,128)(2,1)}, u32[]{:S(2)}) copy-start(bf16[512,1536]{1,0:T(8,128)(2,1)} %k_hbm.1) | copy-start | bytes 4718596
  4.1 1.4 %copy-start.2 = (bf16[512,1536]{1,0:T(8,128)(2,1)S(1)}, bf16[512,1536]{1,0:T(8,128)(2,1)}, u32[]{:S(2)}) copy-start(bf16[512,1536]{1,0:T(8,128)(2,1)} %v_hbm.1) | copy-start | bytes 4718596
  5.6 1.4 %copy-start.3 = (bf16[512,1536]{1,0:T(8,128)(2,1)S(1)}, bf16[512,1536]{1,0:T(8,128)(2,1)}, u32[]{:S(2)}) copy-start(bf16[512,1536]{1,0:T(8,128)(2,1)} %o_hbm.1) | copy-start | bytes 4718596

commit v2 on v1

--- a/solution.py
+++ b/solution.py
@@ -15,6 +15,7 @@
 F32 = jnp.float32
 BF16 = jnp.bfloat16
 LAG = 2
+STORES = 4
 
 
 def dot(a, b, ca, cb):
@@ -32,9 +33,9 @@
 
 def kernel(
     cfg,
-    q_hbm, k_hbm, v_hbm, o_hbm, d_hbm, gain_ref,
+    q_hbm, k_hbm, v_hbm, o_hbm, d_hbm, gain_hbm,
     qg_out, kg_out, vg_out,
-    q_ref, k_ref, v_ref, o_ref, d_ref,
+    q_ref, k_ref, v_ref, o_ref, d_ref, gain_ref,
     acc_q, acc_k, acc_v, terms, slots, zin, inc, sums,
     load_sem, sum_send, sum_recv, y_send, y_recv, z_send, z_recv,
 ):
@@ -46,6 +47,7 @@
     z = seq // ys
     y = seq % ys
     hops = (z, zs - 1 - z)
+    steps = (zs - 1) * 3 // 2 + LAG + n
 
     loads = [
         pltpu.make_async_copy(src, dst, load_sem.at[i])
@@ -55,6 +57,8 @@
     ]
     for load in loads:
         load.start()
+    gain_load = pltpu.make_async_copy(gain_hbm, gain_ref, load_sem.at[5])
+    gain_load.start()
 
     barrier = pltpu.get_barrier_semaphore()
 
@@ -144,9 +148,7 @@
 
         lax.fori_loop(0, n, one, 0)
 
-    def step(kind, t):
-        place = t - hops[kind]
-
+    def step(kind, place):
         @pl.when((place >= 0) & (place < n))
         def _():
             c = lax.rem(place + raw, n)
@@ -174,23 +176,34 @@
                     def _():
                         y_copy(kind, inc.at[kind], c, d).start()
 
-                    @pl.when(jnp.logical_not(later(kind, other)))
+                    @pl.when(jnp.logical_not(later(kind, other)) & (hops[kind] > 0))
                     def _():
                         y_copy(kind, zin.at[kind], c, d).start()
 
             @pl.when(hops[kind] < zs - 1)
             def _():
                 z_copy(kind, c).start()
+
+    def start(kind):
+        first = hops[kind] * 3 // 2 + kind * LAG
+        return jnp.where(hops[kind] == 0, steps, first)
 
     loads[0].wait()
     loads[1].wait()
     peers = hs - 1 + ys - 1 + jnp.where(z > 0, 1, 0) + jnp.where(z < zs - 1, 1, 0)
     pl.semaphore_wait(barrier, peers)
     own_terms(0, k_ref, v_ref)
-    step(0, 0)
+    def ends(kind):
+        @pl.when(hops[kind] == 0)
+        def _():
+            lax.fori_loop(0, n, lambda p, carry: (step(kind, p), carry)[1], 0)
+
+    ends(0)
+    step(0, 0 - start(0))
 
     loads[2].wait()
     loads[3].wait()
+    gain_load.wait()
     tile = 128
     for r in range(rows // tile):
         rs = slice(r * tile, (r + 1) * tile)
@@ -198,7 +211,7 @@
         def partial(h, carry):
             sq, cr = carry
             of = o_ref[rs, lanes(h)].astype(F32)
-            sc = gain_ref[0:1, lanes(h)] * d_ref[rs, lanes(h)].astype(F32)
+            sc = gain_ref[lanes(h)][None, :] * d_ref[rs, lanes(h)].astype(F32)
             return sq + of * of, cr + sc * of
 
         zero = jnp.zeros((tile, DH), F32)
@@ -221,7 +234,7 @@
     for d in range(1, hs):
         sum_copy(mine, d).start()
     for t in range(1, LAG):
-        step(0, t)
+        step(0, t - start(0))
     for d in range(1, hs):
         sum_copy(lax.rem(mine + d, hs), d).wait_recv()
     total = sums[0]
@@ -237,7 +250,7 @@
 
         def normed(h, carry):
             of = o_ref[rs, lanes(h)].astype(F32)
-            sc = gain_ref[0:1, lanes(h)] * d_ref[rs, lanes(h)].astype(F32)
+            sc = gain_ref[lanes(h)][None, :] * d_ref[rs, lanes(h)].astype(F32)
             d_ref[rs, lanes(h)] = (sc * inv - of * coef).astype(BF16)
             return carry
 
@@ -245,6 +258,7 @@
 
     loads[4].wait()
     own_terms(1, q_ref, d_ref)
+    ends(1)
 
     def local(c):
         row = lax.broadcasted_iota(jnp.int32, (GROUP, GROUP), 0)
@@ -264,8 +278,8 @@
                 acc_v[toks(b), lanes(h)] = dot(scores_t, gb, 1, 0)
 
     def turn(t, carry):
-        step(0, t)
-        step(1, t - LAG)
+        step(0, t - start(0))
+        step(1, t - start(1))
 
         @pl.when(t - LAG < n)
         def _():
@@ -273,14 +287,18 @@
 
         return carry
 
-    lax.fori_loop(LAG, n + zs - 1 + LAG, turn, 0)
+    lax.fori_loop(LAG, steps, turn, 0)
 
     def finish(c, carry):
         @pl.when(c >= raw)
         def _():
             for kind in range(2):
                 for d in range(1, ys):
-                    y_arrive(kind, c, d)
+                    other = lax.rem(y + d, ys)
+
+                    @pl.when(jnp.logical_not(later(kind, other)) | (hops[kind] > 0))
+                    def _():
+                        y_arrive(kind, c, d)
 
         for i in range(ch):
             h = c * ch + i
@@ -289,7 +307,7 @@
                 total = zin[kind, h]
                 for d in range(1, ys):
                     other = lax.rem(y + d, ys)
-                    used = jnp.logical_or(c >= raw, jnp.logical_not(later(kind, other)))
+                    used = jnp.logical_not(later(kind, other)) | ((c >= raw) & (hops[kind] > 0))
                     total = total + jnp.where(used, slots[kind, other, h], 0.0)
                 ends.append(total)
             fwd, bwd = [ends[0]], [ends[1]]
@@ -313,7 +331,11 @@
     def sent(c, carry):
         for kind in range(2):
             for d in range(1, ys):
-                y_copy(kind, inc.at[kind], c, d).wait_send()
+                other = lax.rem(y + d, ys)
+
+                @pl.when(later(kind, other) | (c < raw) | (hops[kind] > 0))
+                def _():
+                    y_copy(kind, inc.at[kind], c, d).wait_send()
 
             @pl.when(hops[kind] < zs - 1)
             def _():
@@ -322,6 +344,19 @@
         return carry
 
     lax.fori_loop(0, n, sent, 0)
+
+
+def store_kernel(a, b, c, a_out, b_out, c_out, sem):
+    part = a.shape[0] // STORES
+    copies = []
+    for i in range(STORES):
+        at = slice(i * part, (i + 1) * part)
+        for j, (src, dst) in enumerate(((a, a_out), (b, b_out), (c, c_out))):
+            copies.append(pltpu.make_async_copy(src.at[at], dst.at[at], sem.at[j, i]))
+    for copy in copies:
+        copy.start()
+    for copy in copies:
+        copy.wait()
 
 
 def shards(sizes, queries, keys, values, attn_out, out_grad, norm_gain):
@@ -341,20 +376,21 @@
     out = jax.ShapeDtypeStruct((rows, width), BF16)
     dma = pltpu.SemaphoreType.DMA
     flops = 2 * heads * blocks * (6 * GROUP * GROUP * DH + 5 * GROUP * DH * DH)
-    return pl.pallas_call(
+    held = pl.pallas_call(
         functools.partial(kernel, cfg),
         out_shape=(out, out, out),
-        in_specs=[pl.BlockSpec(memory_space=pl.ANY)] * 5 + [pl.BlockSpec(memory_space=pltpu.VMEM)],
+        in_specs=[pl.BlockSpec(memory_space=pltpu.HBM)] * 6,
         out_specs=[pl.BlockSpec(memory_space=pltpu.VMEM)] * 3,
         scratch_shapes=[
             big, big, big, big, big,
+            pltpu.VMEM((width,), F32),
             acc, acc, acc,
             pltpu.VMEM((2, blocks) + state, F32),
             pltpu.VMEM((2, ys) + state, F32),
             pltpu.VMEM((2,) + state, F32),
             pltpu.VMEM((2,) + state, F32),
             pltpu.VMEM((hs, 8, rows), F32),
-            dma((5,)),
+            dma((6,)),
             dma((hs - 1,)),
             dma((hs,)),
             dma((2, ys - 1, n)),
@@ -368,7 +404,20 @@
         compiler_params=pltpu.CompilerParams(
             collective_id=0, has_side_effects=True, vmem_limit_bytes=42 * 1024 * 1024
         ),
-    )(queries, keys, values, attn_out, out_grad, norm_gain[None, :])
+    )(*[
+        pltpu.with_memory_space_constraint(x, pltpu.HBM)
+        for x in (queries, keys, values, attn_out, out_grad, norm_gain)
+    ])
+    return pl.pallas_call(
+        store_kernel,
+        out_shape=(out, out, out),
+        in_specs=[pl.BlockSpec(memory_space=pltpu.VMEM)] * 3,
+        out_specs=[pl.BlockSpec(memory_space=pltpu.HBM)] * 3,
+        scratch_shapes=[dma((3, STORES))],
+        cost_estimate=pl.CostEstimate(
+            flops=0, bytes_accessed=3 * rows * width * 2, transcendentals=0
+        ),
+    )(*held)
 
 
 def solution(mesh):

time: 60.6 us -> 54.5 us (0.90)
  local copies, waits for them, and re-layouts: 9.76 us -> 3.47 us
    unnamed x11 -> x6, local copies, waits for them, and re-layouts: 9.06 us -> 3.47 us
    pallas_call x0 -> x1, Pallas kernels: none -> 4.62 us  [shards(): pl.pallas_call(store_kernel, out_shape=(out, out, out), in_specs=[pl.Bloc...]
    pallas_call x1, Pallas kernels: 49.9 us -> 45.6 us  [shards(): pl.pallas_call(functools.partial(kernel, cfg), out_shape=(out, out, out),...]
    broadcast_in_dim x1 -> x0, local copies, waits for them, and re-layouts: 0.7 us -> none  [shards(): norm_gain[None, :]]
where the time goes in v2:
time: 54.5 us; the launch traced here: 54.4 us
  Pallas kernels  50.2 us (92%)
  local copies, waits for them, and re-layouts  3.47 us (6%)
  between operations  0.65 us (1%)
    pallas_call x1, Pallas kernels, shards(): pl.pallas_call(functools.partial(kernel, cfg), out_shape=(out, out, out),...  45.6 us
    pallas_call x1, Pallas kernels, shards(): pl.pallas_call(store_kernel, out_shape=(out, out, out), in_specs=[pl.Bloc...  4.62 us
    unnamed x6, local copies, waits for them, and re-layouts  3.47 us

profile of v2, /device:TPU:0, one launch (start us, length us, event | category | flops | bytes accessed | tf_op | source)
XLA Modules:
  0.0 54.4 jit_solution(7888823150882838152)
XLA Ops:
  0.6 45.6 %shard_map.85 = (bf16[512,1536]{1,0:T(8,128)(2,1)S(1)}, bf16[512,1536]{1,0:T(8,128)(2,1)S(1)}, bf16[512,1536]{1,0:T(8,128)(2,1)S(1)}) custom-call(bf16[512,1536]{1,0:T(8,128)(2,1)} %q_hbm.1, bf16[512,1536]{1,0:T(8,128)(2,1)} %k_hbm.1, bf16[512,1536]{1,0:T(8,128)(2,1)} %v_hbm.1, bf16[512,1536]{1,0:T(8,128)(2,1)} %o_hbm.1, bf16[512,1536]{1,0:T(8,128)(2,1)} %d_hbm.1, ...), custom_call_target="tpu_custom_call" | custom-call | flops 3422552064 | bytes 12582912 | tf_op jit(solution)/shard_map/pallas_call | solution.py:379
  46.3 0.0 copy-start
  46.3 1.2 %copy-done = bf16[512,1536]{1,0:T(8,128)(2,1)} copy-done((bf16[512,1536]{1,0:T(8,128)(2,1)}, bf16[512,1536]{1,0:T(8,128)(2,1)S(1)}, u32[]{:S(2)}) %copy-start) | copy-done | bytes 1572888
  47.4 0.0 copy-start.1
  47.4 1.2 %copy-done.1 = bf16[512,1536]{1,0:T(8,128)(2,1)} copy-done((bf16[512,1536]{1,0:T(8,128)(2,1)}, bf16[512,1536]{1,0:T(8,128)(2,1)S(1)}, u32[]{:S(2)}) %copy-start.1) | copy-done | bytes 1572888
  48.6 0.0 copy-start.2
  48.6 1.1 %copy-done.2 = bf16[512,1536]{1,0:T(8,128)(2,1)} copy-done((bf16[512,1536]{1,0:T(8,128)(2,1)}, bf16[512,1536]{1,0:T(8,128)(2,1)S(1)}, u32[]{:S(2)}) %copy-start.2) | copy-done | bytes 1572888
  49.7 4.6 %shard_map.86 = (bf16[512,1536]{1,0:T(8,128)(2,1)}, bf16[512,1536]{1,0:T(8,128)(2,1)}, bf16[512,1536]{1,0:T(8,128)(2,1)}) custom-call(bf16[512,1536]{1,0:T(8,128)(2,1)} %copy-done, bf16[512,1536]{1,0:T(8,128)(2,1)} %copy-done.1, bf16[512,1536]{1,0:T(8,128)(2,1)} %copy-done.2), custom_call_target="tpu_custom_call" | custom-call | bytes 4718592 | tf_op jit(solution)/shard_map/pallas_call | solution.py:411
Async XLA Ops:
  46.3 1.2 %copy-start = (bf16[512,1536]{1,0:T(8,128)(2,1)}, bf16[512,1536]{1,0:T(8,128)(2,1)S(1)}, u32[]{:S(2)}) copy-start(bf16[512,1536]{1,0:T(8,128)(2,1)S(1)} %get-tuple-element.6.a) | copy-start | bytes 4718596
  47.4 1.2 %copy-start.1 = (bf16[512,1536]{1,0:T(8,128)(2,1)}, bf16[512,1536]{1,0:T(8,128)(2,1)S(1)}, u32[]{:S(2)}) copy-start(bf16[512,1536]{1,0:T(8,128)(2,1)S(1)} %get-tuple-element.7.b) | copy-start | bytes 4718596
  48.6 1.2 %copy-start.2 = (bf16[512,1536]{1,0:T(8,128)(2,1)}, bf16[512,1536]{1,0:T(8,128)(2,1)S(1)}, u32[]{:S(2)}) copy-start(bf16[512,1536]{1,0:T(8,128)(2,1)S(1)} %get-tuple-element.8.c) | copy-start | bytes 4718596

commit v3 on v2

--- a/solution.py
+++ b/solution.py
@@ -14,7 +14,10 @@
 MESH = pl.DeviceIdType.MESH
 F32 = jnp.float32
 BF16 = jnp.bfloat16
-LAG = 2
+LAG = 4
+EARLY = 3
+HOP = 2
+SETTLE = 3
 STORES = 4
 
 
@@ -47,7 +50,7 @@
     z = seq // ys
     y = seq % ys
     hops = (z, zs - 1 - z)
-    steps = (zs - 1) * 3 // 2 + LAG + n
+    steps = (zs - 1) * HOP + LAG + n
 
     loads = [
         pltpu.make_async_copy(src, dst, load_sem.at[i])
@@ -185,8 +188,8 @@
                 z_copy(kind, c).start()
 
     def start(kind):
-        first = hops[kind] * 3 // 2 + kind * LAG
-        return jnp.where(hops[kind] == 0, steps, first)
+        first = hops[kind] * HOP + kind * LAG
+        return jnp.where(hops[kind] == 0, steps + SETTLE, first)
 
     loads[0].wait()
     loads[1].wait()
@@ -233,7 +236,7 @@
 
     for d in range(1, hs):
         sum_copy(mine, d).start()
-    for t in range(1, LAG):
+    for t in range(1, EARLY):
         step(0, t - start(0))
     for d in range(1, hs):
         sum_copy(lax.rem(mine + d, hs), d).wait_recv()
@@ -277,19 +280,7 @@
                 scores_t = jnp.where(col >= row, dot(kb, qb, 1, 1), 0.0).astype(BF16)
                 acc_v[toks(b), lanes(h)] = dot(scores_t, gb, 1, 0)
 
-    def turn(t, carry):
-        step(0, t - start(0))
-        step(1, t - start(1))
-
-        @pl.when(t - LAG < n)
-        def _():
-            local(t - LAG)
-
-        return carry
-
-    lax.fori_loop(LAG, steps, turn, 0)
-
-    def finish(c, carry):
+    def finish(c):
         @pl.when(c >= raw)
         def _():
             for kind in range(2):
@@ -321,9 +312,39 @@
                 qg_out[at] = ((acc_q[at] + dot(gb, fs, 1, 1)) * factor).astype(BF16)
                 kg_out[at] = ((acc_k[at] + dot(vb, bs, 1, 1)) * factor).astype(BF16)
                 vg_out[at] = ((acc_v[at] + dot(kb, bs, 1, 0)) * factor).astype(BF16)
+
+    last = jnp.maximum(
+        jnp.where(hops[0] > 0, hops[0] * HOP, 0), jnp.where(hops[1] > 0, hops[1] * HOP + LAG, 0)
+    )
+    edge = (hops[0] == 0) | (hops[1] == 0)
+
+    def turn(t, carry):
+        step(0, t - start(0))
+        step(1, t - start(1))
+
+        @pl.when(t - EARLY < n)
+        def _():
+            local(t - EARLY)
+
+        place = t - last
+
+        @pl.when((place >= n - raw) & (place < n))
+        def _():
+            finish(lax.rem(place + raw, n))
+
+        settled = place - SETTLE
+
+        @pl.when(edge & (settled >= 0) & (settled < n - raw))
+        def _():
+            finish(settled + raw)
+
         return carry
 
-    lax.fori_loop(0, n, finish, 0)
+    lax.fori_loop(EARLY, steps + SETTLE, turn, 0)
+
+    @pl.when(jnp.logical_not(edge))
+    def _():
+        lax.fori_loop(raw, n, lambda c, carry: (finish(c), carry)[1], 0)
 
     for d in range(1, hs):
         sum_copy(mine, d).wait_send()
@@ -365,9 +386,9 @@
     rows, width = queries.shape
     heads = width // DH
     blocks = rows // GROUP
-    ch = 2 if heads % 2 == 0 else 1
+    ch = 1
     n = heads // ch
-    raw = n // 3
+    raw = n // 2
     factor = 1.0 / math.sqrt(DH * rows * seqs)
     cfg = (zs, ys, hs, heads, ch, raw, rows, width * hs, factor)
     big = pltpu.VMEM((rows, width), BF16)
@@ -411,12 +432,13 @@
     return pl.pallas_call(
         store_kernel,
         out_shape=(out, out, out),
-        in_specs=[pl.BlockSpec(memory_space=pltpu.VMEM)] * 3,
+        in_specs=[pl.BlockSpec(memory_space=pl.ANY)] * 3,
         out_specs=[pl.BlockSpec(memory_space=pltpu.HBM)] * 3,
         scratch_shapes=[dma((3, STORES))],
         cost_estimate=pl.CostEstimate(
             flops=0, bytes_accessed=3 * rows * width * 2, transcendentals=0
         ),
+        compiler_params=pltpu.CompilerParams(vmem_limit_bytes=4 * 1024 * 1024),
     )(*held)
 
 

time: 54.5 us -> 48.8 us (0.90)
  local copies, waits for them, and re-layouts: 3.47 us -> 0 us
  Pallas kernels: 50.2 us -> 48 us
    unnamed x6 -> x0, local copies, waits for them, and re-layouts: 3.47 us -> none
    pallas_call x1, Pallas kernels: 4.62 us -> 2.27 us  [shards(): pl.pallas_call(store_kernel, out_shape=(out, out, out), in_specs=[pl.Bloc...]
where the time goes in v3:
time: 48.8 us; the launch traced here: 48.7 us
  Pallas kernels  48 us (98%)
  between operations  0.64 us (1%)
    pallas_call x1, Pallas kernels, shards(): pl.pallas_call(functools.partial(kernel, cfg), out_shape=(out, out, out),...  45.7 us
    pallas_call x1, Pallas kernels, shards(): pl.pallas_call(store_kernel, out_shape=(out, out, out), in_specs=[pl.Bloc...  2.27 us

profile of v3, /device:TPU:0, one launch (start us, length us, event | category | flops | bytes accessed | tf_op | source)
XLA Modules:
  0.0 48.7 jit_solution(3640063453773474899)
XLA Ops:
  0.6 45.7 %shard_map.85 = (bf16[512,1536]{1,0:T(8,128)(2,1)S(1)}, bf16[512,1536]{1,0:T(8,128)(2,1)S(1)}, bf16[512,1536]{1,0:T(8,128)(2,1)S(1)}) custom-call(bf16[512,1536]{1,0:T(8,128)(2,1)} %q_hbm.1, bf16[512,1536]{1,0:T(8,128)(2,1)} %k_hbm.1, bf16[512,1536]{1,0:T(8,128)(2,1)} %v_hbm.1, bf16[512,1536]{1,0:T(8,128)(2,1)} %o_hbm.1, bf16[512,1536]{1,0:T(8,128)(2,1)} %d_hbm.1, ...), custom_call_target="tpu_custom_call" | custom-call | flops 3422552064 | bytes 12582912 | tf_op jit(solution)/shard_map/pallas_call | solution.py:400
  46.4 2.3 %shard_map.86 = (bf16[512,1536]{1,0:T(8,128)(2,1)}, bf16[512,1536]{1,0:T(8,128)(2,1)}, bf16[512,1536]{1,0:T(8,128)(2,1)}) custom-call(bf16[512,1536]{1,0:T(8,128)(2,1)S(1)} %get-tuple-element.6.a, bf16[512,1536]{1,0:T(8,128)(2,1)S(1)} %get-tuple-element.7.b, bf16[512,1536]{1,0:T(8,128)(2,1)S(1)} %get-tuple-element.8.c), custom_call_target="tpu_custom_call" | custom-call | bytes 4718592 | tf_op jit(solution)/shard_map/pallas_call | solution.py:432

commit v4 on v3

--- a/solution.py
+++ b/solution.py
@@ -14,8 +14,7 @@
 MESH = pl.DeviceIdType.MESH
 F32 = jnp.float32
 BF16 = jnp.bfloat16
-LAG = 4
-EARLY = 3
+LAG = 1
 HOP = 2
 SETTLE = 3
 STORES = 4
@@ -55,7 +54,7 @@
     loads = [
         pltpu.make_async_copy(src, dst, load_sem.at[i])
         for i, (src, dst) in enumerate(
-            ((k_hbm, k_ref), (v_hbm, v_ref), (o_hbm, o_ref), (d_hbm, d_ref), (q_hbm, q_ref))
+            ((o_hbm, o_ref), (d_hbm, d_ref), (k_hbm, k_ref), (v_hbm, v_ref), (q_hbm, q_ref))
         )
     ]
     for load in loads:
@@ -131,6 +130,9 @@
     def later(kind, other):
         return other > y if kind == 0 else other < y
 
+    def raw_sent(kind, d):
+        return later(kind, lax.rem(y + d, ys)) | (hops[kind] < zs - 1)
+
     def own_terms(kind, a_ref, b_ref):
         def one(c, carry):
             for i in range(ch):
@@ -145,14 +147,21 @@
             @pl.when(c < raw)
             def _():
                 for d in range(1, ys):
-                    y_copy(kind, slots.at[kind, y], c, d).start()
+
+                    @pl.when(raw_sent(kind, d))
+                    def _():
+                        y_copy(kind, slots.at[kind, y], c, d).start()
+
+            @pl.when((c >= raw) & (hops[kind] == 0))
+            def _():
+                step(kind, c - raw, 0)
 
             return carry
 
         lax.fori_loop(0, n, one, 0)
 
-    def step(kind, place):
-        @pl.when((place >= 0) & (place < n))
+    def step(kind, place, first):
+        @pl.when((place >= first) & (place < n))
         def _():
             c = lax.rem(place + raw, n)
 
@@ -163,11 +172,18 @@
             @pl.when(place >= n - raw)
             def _():
                 for d in range(1, ys):
-                    y_arrive(kind, c, d)
-                total = zin[kind, chunk(c)]
-                for s in range(ys):
-                    total = total + slots[kind, s, chunk(c)]
-                inc[kind, chunk(c)] = total
+                    other = lax.rem(y + d, ys)
+
+                    @pl.when(jnp.logical_not(later(kind, other)) | (hops[kind] < zs - 1))
+                    def _():
+                        y_arrive(kind, c, d)
+
+                @pl.when(hops[kind] < zs - 1)
+                def _():
+                    total = zin[kind, chunk(c)]
+                    for s in range(ys):
+                        total = total + slots[kind, s, chunk(c)]
+                    inc[kind, chunk(c)] = total
 
             @pl.when(place < n - raw)
             def _():
@@ -188,24 +204,10 @@
                 z_copy(kind, c).start()
 
     def start(kind):
-        first = hops[kind] * HOP + kind * LAG
-        return jnp.where(hops[kind] == 0, steps + SETTLE, first)
+        return hops[kind] * HOP + kind * LAG
 
     loads[0].wait()
     loads[1].wait()
-    peers = hs - 1 + ys - 1 + jnp.where(z > 0, 1, 0) + jnp.where(z < zs - 1, 1, 0)
-    pl.semaphore_wait(barrier, peers)
-    own_terms(0, k_ref, v_ref)
-    def ends(kind):
-        @pl.when(hops[kind] == 0)
-        def _():
-            lax.fori_loop(0, n, lambda p, carry: (step(kind, p), carry)[1], 0)
-
-    ends(0)
-    step(0, 0 - start(0))
-
-    loads[2].wait()
-    loads[3].wait()
     gain_load.wait()
     tile = 128
     for r in range(rows // tile):
@@ -234,10 +236,15 @@
             device_id_type=MESH,
         )
 
+    peers = hs - 1 + ys - 1 + jnp.where(z > 0, 1, 0) + jnp.where(z < zs - 1, 1, 0)
+    pl.semaphore_wait(barrier, peers)
     for d in range(1, hs):
         sum_copy(mine, d).start()
-    for t in range(1, EARLY):
-        step(0, t - start(0))
+
+    loads[2].wait()
+    loads[3].wait()
+    own_terms(0, k_ref, v_ref)
+
     for d in range(1, hs):
         sum_copy(lax.rem(mine + d, hs), d).wait_recv()
     total = sums[0]
@@ -261,7 +268,6 @@
 
     loads[4].wait()
     own_terms(1, q_ref, d_ref)
-    ends(1)
 
     def local(c):
         row = lax.broadcasted_iota(jnp.int32, (GROUP, GROUP), 0)
@@ -313,18 +319,16 @@
                 kg_out[at] = ((acc_k[at] + dot(vb, bs, 1, 1)) * factor).astype(BF16)
                 vg_out[at] = ((acc_v[at] + dot(kb, bs, 1, 0)) * factor).astype(BF16)
 
-    last = jnp.maximum(
-        jnp.where(hops[0] > 0, hops[0] * HOP, 0), jnp.where(hops[1] > 0, hops[1] * HOP + LAG, 0)
-    )
+    last = jnp.maximum(start(0), start(1))
     edge = (hops[0] == 0) | (hops[1] == 0)
 
     def turn(t, carry):
-        step(0, t - start(0))
-        step(1, t - start(1))
-
-        @pl.when(t - EARLY < n)
-        def _():
-            local(t - EARLY)
+        for kind in range(2):
+            step(kind, t - start(kind), jnp.where(hops[kind] == 0, n - raw, 0))
+
+        @pl.when(t < n)
+        def _():
+            local(t)
 
         place = t - last
 
@@ -340,7 +344,7 @@
 
         return carry
 
-    lax.fori_loop(EARLY, steps + SETTLE, turn, 0)
+    lax.fori_loop(0, steps + SETTLE, turn, 0)
 
     @pl.when(jnp.logical_not(edge))
     def _():
@@ -354,7 +358,9 @@
             for d in range(1, ys):
                 other = lax.rem(y + d, ys)
 
-                @pl.when(later(kind, other) | (c < raw) | (hops[kind] > 0))
+                begun = jnp.where(c < raw, hops[kind] < zs - 1, hops[kind] > 0)
+
+                @pl.when(later(kind, other) | begun)
                 def _():
                     y_copy(kind, inc.at[kind], c, d).wait_send()
 

time: 48.8 us -> 52 us (1.066)
  Pallas kernels: 48 us -> 51.2 us
    pallas_call x1, Pallas kernels: 45.7 us -> 48.9 us  [shards(): pl.pallas_call(functools.partial(kernel, cfg), out_shape=(out, out, out),...]
where the time goes in v4:
time: 52 us; the launch traced here: 51.8 us
  Pallas kernels  51.2 us (98%)
  between operations  0.64 us (1%)
    pallas_call x1, Pallas kernels, shards(): pl.pallas_call(functools.partial(kernel, cfg), out_shape=(out, out, out),...  48.9 us
    pallas_call x1, Pallas kernels, shards(): pl.pallas_call(store_kernel, out_shape=(out, out, out), in_specs=[pl.Bloc...  2.27 us

profile of v4, /device:TPU:0, one launch (start us, length us, event | category | flops | bytes accessed | tf_op | source)
XLA Modules:
  0.0 51.8 jit_solution(14279146455645192740)
XLA Ops:
  0.6 48.9 %shard_map.85 = (bf16[512,1536]{1,0:T(8,128)(2,1)S(1)}, bf16[512,1536]{1,0:T(8,128)(2,1)S(1)}, bf16[512,1536]{1,0:T(8,128)(2,1)S(1)}) custom-call(bf16[512,1536]{1,0:T(8,128)(2,1)} %q_hbm.1, bf16[512,1536]{1,0:T(8,128)(2,1)} %k_hbm.1, bf16[512,1536]{1,0:T(8,128)(2,1)} %v_hbm.1, bf16[512,1536]{1,0:T(8,128)(2,1)} %o_hbm.1, bf16[512,1536]{1,0:T(8,128)(2,1)} %d_hbm.1, ...), custom_call_target="tpu_custom_call" | custom-call | flops 3422552064 | bytes 12582912 | tf_op jit(solution)/shard_map/pallas_call | solution.py:406
  49.6 2.3 %shard_map.86 = (bf16[512,1536]{1,0:T(8,128)(2,1)}, bf16[512,1536]{1,0:T(8,128)(2,1)}, bf16[512,1536]{1,0:T(8,128)(2,1)}) custom-call(bf16[512,1536]{1,0:T(8,128)(2,1)S(1)} %get-tuple-element.6.a, bf16[512,1536]{1,0:T(8,128)(2,1)S(1)} %get-tuple-element.7.b, bf16[512,1536]{1,0:T(8,128)(2,1)S(1)} %get-tuple-element.8.c), custom_call_target="tpu_custom_call" | custom-call | bytes 4718592 | tf_op jit(solution)/shard_map/pallas_call | solution.py:438
